TPU v7x, 128 devices: a whole 4x4x4 slice. The times are simulated.
128 devices in a mesh: row: 128 (over y, x, z, core).
Axes of the slice: x: 4, y: 4, z: 4, core: 2. Of those that a mesh axis runs over, the one named last changes fastest.
Arguments:
- matrix_blocks: bfloat16 [256, 48, 256, 256], P('row'), may hold values from -0.078125 to 0.078125
- test_panel: bfloat16 [65536, 256], P('row'), may hold values from -6 to 6
- column_blocks: int32 [256, 48], P('row'), may hold values from 0 to 255, as said below
- row_counts: int32 [256], P('row'), may hold values from 16 to 48, as said below
Outputs:
- basis: float32 [65536, 256], P('row')
- triangle: float32 [256, 256], replicated
Inputs may be any that keep to these rules, and one draw needn't show every extreme that they name: `column_blocks`: block column indices of all slots, padding slots too. Among the slots of the 2 block rows of one device, at most 1 have a column block in the 2 block rows held by any one device (block c is held by device c // 2), and the first slot of each device's first block row is always live (every row has at least 16 live slots). `row_counts`: live slots per block row; some block row is full.
All inputs are finite; a program needn't handle non-finite values.
Results may differ from a plain program's by a relative error of at most 0.0003.
Values may be sent and summed in bfloat16 or wider, within the bound.
A program may use at most 192 MiB of HBM per device.

v0:
```python
import math

import jax
import jax.numpy as jnp
from jax import lax
from jax.sharding import PartitionSpec as P


def factor_pair(gram):
    highest = lax.Precision.HIGHEST
    order = gram.shape[0]
    index = jnp.arange(order, dtype=jnp.int32)

    def column_step(column, carry):
        lower, inverse = carry
        row_now = lax.dynamic_slice_in_dim(lower, column, 1, 0)[0]
        current = lax.dynamic_slice_in_dim(gram, column, 1, 1)[:, 0] - jnp.dot(
            lower, row_now, precision=highest
        )
        pivot = jnp.sqrt(lax.dynamic_slice_in_dim(current, column, 1, 0)[0])
        filled = jnp.where(index >= column, current / pivot, jnp.float32(0.0))
        pick = (index == column).astype(jnp.float32)
        lower = lower + filled[:, None] * pick[None, :]
        row_now = lax.dynamic_slice_in_dim(lower, column, 1, 0)[0]
        inverse_row = (pick - jnp.dot(row_now, inverse, precision=highest)) / pivot
        inverse = inverse + pick[:, None] * inverse_row[None, :]
        return (lower, inverse)

    start = jnp.zeros((order, order), jnp.float32)
    lower, inverse = lax.fori_loop(0, order, column_step, (start, start))
    return (lower.T, inverse.T)


def right_solve(inverse, values):
    return jnp.dot(values, inverse, precision=lax.Precision.HIGHEST)


def per_device(matrix_blocks, test_panel, column_blocks, row_counts):
    rows_here, width_slots, block_size, _ = matrix_blocks.shape
    panel_cols = test_panel.shape[1]
    devices = lax.axis_size("row")
    slot_total = rows_here * width_slots
    capacity = (slot_total + devices - 1) // devices
    panel = test_panel.reshape(rows_here, block_size, panel_cols)
    flat_cols = column_blocks.reshape(slot_total)
    positions = jnp.arange(width_slots, dtype=jnp.int32)
    alive = (positions[None, :] < row_counts[:, None]).reshape(slot_total)
    owners = flat_cols // rows_here
    within = flat_cols % rows_here
    order = jnp.arange(slot_total, dtype=jnp.int32)
    earlier = (
        (owners[:, None] == owners[None, :]) & alive[None, :] & (order[None, :] < order[:, None])
    )
    slot_rank = jnp.sum(earlier.astype(jnp.int32), axis=1)
    target = jnp.where(alive, owners * capacity + slot_rank, devices * capacity)
    wanted = jnp.full((devices * capacity,), -1, jnp.int32).at[target].set(within, mode="drop")
    asked = lax.all_to_all(
        wanted.reshape(devices, capacity), "row", split_axis=0, concat_axis=0, tiled=True
    )
    reply = jnp.take(panel, jnp.maximum(asked, 0), axis=0)
    reply = jnp.where((asked >= 0)[:, :, None, None], reply, jnp.zeros_like(reply))
    arrived = lax.all_to_all(reply, "row", split_axis=0, concat_axis=0, tiled=True)
    arrived = arrived.reshape(devices * capacity, block_size, panel_cols)
    picked = jnp.take(arrived, jnp.minimum(target, devices * capacity - 1), axis=0)
    picked = jnp.where(alive[:, None, None], picked, jnp.zeros_like(picked))
    picked = picked.reshape(rows_here, width_slots, block_size, panel_cols)
    sample = jnp.einsum("rbij,rbjk->rik", matrix_blocks, picked, preferred_element_type=jnp.float32)
    sample = sample.reshape(rows_here * block_size, panel_cols)
    highest = lax.Precision.HIGHEST
    gram = lax.psum(jnp.dot(sample.T, sample, precision=highest), "row")
    factor, inverse = factor_pair(gram)
    ortho = right_solve(inverse, sample)
    scale = math.sqrt(devices * rows_here * block_size)
    return (ortho * scale, factor / scale)


def solution(mesh):
    in_specs = (P("row", None, None, None), P("row", None), P("row", None), P("row"))
    out_specs = (P("row", None), P())
    return jax.shard_map(
        per_device, mesh=mesh, in_specs=in_specs, out_specs=out_specs, check_vma=False
    )
```

profile of v0, /device:TPU:1, one launch (start us, length us, event | category | flops | bytes accessed | tf_op | source)
XLA Modules:
  0.0 1037.4 jit_solution(2834282721060066208)
XLA Ops:
  7.2 0.8 iota_compare_fusion.1
  8.1 0.8 reshape.301
  8.9 0.8 reshape.302
  9.9 0.9 scatter_custom_fusion
  10.9 20.7 %all_to_all.14 = s32[128,1,1]{2,1,0:T(1,128)S(1)} all-to-all(s32[128,1,1]{2,1,0:T(1,128)S(1)} %copy.19), channel_id=1, replica_groups=mesh['row'=128] {'row'}, dimensions={0} | all-to-all | bytes 1024 | tf_op jit(solution)/shard_map/all_to_all | solution.py:57
  31.6 2.4 maximum_reduce_fusion
  33.9 7.8 gather_fusion
  41.8 4.6 compare_reduce_fusion.1
  46.4 14.4 %fusion.14 = bf16[128,1,256,256]{3,2,1,0:T(8,128)(2,1)} fusion(bf16[128,256,256]{2,1,0:T(8,128)(2,1)} %gather_fusion, pred[128]{0:T(512)(128)(4,1)S(1)} %get-tuple-element.150, pred[128]{0:T(512)(128)(4,1)S(1)} %get-tuple-element.149), kind=kLoop, calls=%fused_computation.24 | loop fusion | flops 16777216 | bytes 33554688 | tf_op jit(solution)/shard_map/jit(_where)/select_n | solution.py:61
  60.8 6.0 all-to-all-start.1
  67.2 220.3 %all-to-all-done.1 = bf16[128,1,256,256]{3,2,1,0:T(8,128)(2,1)} async-done(((bf16[128,1,256,256]{3,2,1,0:T(8,128)(2,1)}), bf16[128,1,256,256]{3,2,1,0:T(8,128)(2,1)}, u32[]{:S(2)}, u32[]{:S(2)}) %all-to-all-start.1) | async-done | bytes 16777248 | tf_op jit(solution)/shard_map/all_to_all | solution.py:62
  287.5 12.6 %gather_fusion.1 = bf16[96,256,256]{2,1,0:T(8,128)(2,1)} fusion(bf16[128,256,256]{2,1,0:T(8,128)(2,1)} %bitcast.5, s32[1024]{0:T(1024)S(1)} %pad_clamp_fusion), kind=kCustom, calls=%fused_computation.1 | custom fusion | bytes 25166208 | tf_op jit(solution)/shard_map/jit(_take)/gather | solution.py:64
  300.2 10.1 fusion.15
  310.3 1.7 convolution_bitcast_fusion
  312.1 154.5 %all-reduce.2.cloned.1.call-done = f32[256,256]{1,0:T(8,128)} async-done(((f32[256,256]{1,0:T(8,128)}), f32[256,256]{1,0:T(8,128)}) %all-reduce.2.cloned.1.call-update) | async-done | bytes 262160 | tf_op jit(solution)/shard_map/psum | solution.py:70
  466.6 1.1 copy.21
  467.7 560.6 %while.17 = (s32[]{:T(128)}, f32[256,256]{1,0:T(8,128)S(1)}, f32[256,256]{1,0:T(8,128)S(1)}, f32[256,256]{0,1:T(8,128)S(1)}, s32[]{:T(128)}, /*index=5*/s32[]{:T(128)}) while((s32[]{:T(128)}, f32[256,256]{1,0:T(8,128)S(1)}, f32[256,256]{1,0:T(8,128)S(1)}, f32[256,256]{0,1:T(8,128)S(1)}, s32[]{:T(128)}, ...), condition=%wide.region_4.5_spmd.clone.clone, body=%wide.region_3.4_spmd.clone.clone.sunk | while | flops 2099715 | bytes 2115718 | solution.py:30
  468.1 0.6 dynamic_slice.52
  470.2 0.6 dynamic_slice.52
  472.4 0.6 dynamic_slice.52
  474.6 0.6 dynamic_slice.52
  476.8 0.6 dynamic_slice.52
  479.0 0.6 dynamic_slice.52
  481.2 0.6 dynamic_slice.52
  483.4 0.6 dynamic_slice.52
  485.6 0.6 dynamic_slice.52
  487.8 0.6 dynamic_slice.52
  490.0 0.6 dynamic_slice.52
  492.1 0.6 dynamic_slice.52
  494.3 0.6 dynamic_slice.52
  496.5 0.6 dynamic_slice.52
  498.7 0.6 dynamic_slice.52
  500.9 0.6 dynamic_slice.52
  503.1 0.6 dynamic_slice.52
  505.3 0.6 dynamic_slice.52
  507.5 0.6 dynamic_slice.52
  509.7 0.6 dynamic_slice.52
  511.9 0.6 dynamic_slice.52
  514.0 0.6 dynamic_slice.52
  516.2 0.6 dynamic_slice.52
  518.4 0.6 dynamic_slice.52
  520.6 0.6 dynamic_slice.52
  522.8 0.6 dynamic_slice.52
  525.0 0.6 dynamic_slice.52
  527.2 0.6 dynamic_slice.52
  529.4 0.6 dynamic_slice.52
  531.6 0.6 dynamic_slice.52
  533.8 0.6 dynamic_slice.52
  535.9 0.6 dynamic_slice.52
  538.1 0.6 dynamic_slice.52
  540.3 0.6 dynamic_slice.52
  542.5 0.6 dynamic_slice.52
  544.7 0.6 dynamic_slice.52
  546.9 0.6 dynamic_slice.52
  549.1 0.6 dynamic_slice.52
  551.3 0.6 dynamic_slice.52
  553.5 0.6 dynamic_slice.52
  555.7 0.6 dynamic_slice.52
  557.8 0.6 dynamic_slice.52
  560.0 0.6 dynamic_slice.52
  562.2 0.6 dynamic_slice.52
  564.4 0.6 dynamic_slice.52
  1028.4 0.7 multiply_bitcast_fusion
  1029.2 1.4 convolution_multiply_fusion
  (2795 shorter events, 337.1 us)
Async XLA Ops:
  7.2 26.8 %copy-start = (bf16[512,256]{1,0:T(8,128)(2,1)S(1)}, bf16[512,256]{1,0:T(8,128)(2,1)}, u32[]{:S(2)}) copy-start(bf16[512,256]{1,0:T(8,128)(2,1)} %param.7) | copy-start | bytes 786436
  60.8 6.3 copy-start.2
  60.8 6.3 copy-start.3
  60.8 226.7 %all-to-all-start.1 = ((bf16[128,1,256,256]{3,2,1,0:T(8,128)(2,1)}), bf16[128,1,256,256]{3,2,1,0:T(8,128)(2,1)}, u32[]{:S(2)}, u32[]{:S(2)}) async-start(bf16[128,1,256,256]{3,2,1,0:T(8,128)(2,1)} %fusion.14), calls=%async_computation.1 | async-start | bytes 33554432 | tf_op jit(solution)/shard_map/all_to_all | solution.py:62
  66.8 399.8 %all-reduce.2.cloned.1.call-start = ((), (), s32[]{:S(2)}) async-start(), calls=%async_computation.2 | async-start | bytes 524288 | tf_op jit(solution)/shard_map/psum | solution.py:70
  300.2 730.4 %copy-start.1 = (bf16[512,256]{1,0:T(8,128)(2,1)S(1)}, bf16[512,256]{1,0:T(8,128)(2,1)}, u32[]{:S(2)}) copy-start(bf16[512,256]{1,0:T(8,128)(2,1)} %param.7) | copy-start | bytes 786436
Sparse Core Ops, SparseCore 0:
  312.2 154.3 all-reduce.1
where the time goes:
time: 1040 us
  waiting for transfers between devices  375 us (36%)
  loops' own time  198 us (19%)
  local copies, waits for them, and re-layouts  191 us (18%)
  matrix products  133 us (13%)
  other arithmetic  99 us (10%)
  blocking collectives  20.7 us (2%)
  between operations  14.1 us (1%)
    all_to_all x1, waiting for transfers between devices, per_device(): lax.all_to_all(reply, 'row', split_axis=0, concat_axis=0, tiled=True)  220 us
    another operation x1, loops' own time, factor_pair(): lower, inverse = lax.fori_loop(0, order, column_step, (start, start))  198 us
    psum x1, waiting for transfers between devices, per_device(): gram = lax.psum(jnp.dot(sample.T, sample, precision=highest), 'row')  154 us
    dynamic_slice x256, local copies, waits for them, and re-layouts, column_step(): pivot = jnp.sqrt(lax.dynamic_slice_in_dim(current, column, 1, 0)[0])  151 us
    dot_general x256, matrix products, column_step(): jnp.dot(lower, row_now, precision=highest)  67.9 us
    dot_general x256, matrix products, column_step(): inverse_row = (pick - jnp.dot(row_now, inverse, precision=highest)) / pivot  52.1 us
    add x256, other arithmetic, column_step(): inverse = inverse + pick[:, None] * inverse_row[None, :]  29.6 us
    add x256, other arithmetic, column_step(): lower = lower + filled[:, None] * pick[None, :]  28.6 us
  transfers between devices with their start and end apart: 2, of which 2 were waited for; matrix products, arithmetic and copies ran while one was open for 0% of the time, Pallas kernels for 0%

commit v1 on v0

v1 whole, which is shorter than its diff:
```python
import functools

import jax
import jax.numpy as jnp
from jax import lax
from jax.experimental import pallas as pl
from jax.experimental.pallas import tpu as pltpu
from jax.sharding import PartitionSpec as P

MESH = pl.DeviceIdType.MESH
HI = lax.Precision.HIGHEST


PIECES = ((0, 176), (176, 176), (352, 160))
HALF = (96, 80, 80)
STEP = (0, 3, 1, 2)
N_COPIES = 156
GROUP = 6


def sample_kernel(cols_ref, counts_ref, blocks_ref, panel_ref, sample_ref, gram_ref, panels, held, table_v, table_s, local, twin_half, terms, send_sem, recv_sem, local_sem, line_send, line_recv, pair_send, pair_recv):
    me = lax.axis_index("row")
    core = me % 2
    coords = [me // 32, (me // 8) % 4, (me // 2) % 4]

    def device(at, which):
        return at[0] * 32 + at[1] * 8 + at[2] * 2 + which

    def shifted(axis, by):
        at = list(coords)
        at[axis] = (at[axis] + by) % 4
        return at

    sibling = device(coords, 1 - core)
    partners = [device(shifted(a, s), core) for a in range(3) for s in (1, 2, 3)] + [sibling]
    barrier = pltpu.get_barrier_semaphore()
    for other in partners:
        pl.semaphore_signal(barrier, inc=1, device_id=(other,), device_id_type=MESH)
    blocks_copy = pltpu.make_async_copy(blocks_ref, held, local_sem.at[0])
    blocks_copy.start()
    own = pltpu.make_async_copy(panel_ref, panels.at[coords[0], coords[1], coords[2], core], local_sem.at[1])
    own.start()
    pl.semaphore_wait(barrier, len(partners))

    started = []
    landed = {}

    def view(where, rows, which=core):
        return panels.at[where[0], where[1], where[2], which, pl.ds(rows[0], rows[1])]

    def push(key, src, dst, target):
        slot = len(started)
        copy = pltpu.make_async_remote_copy(
            src_ref=src, dst_ref=dst, send_sem=send_sem.at[slot], recv_sem=recv_sem.at[slot],
            device_id=(target,), device_id_type=MESH)
        copy.start()
        started.append(copy)
        landed[key] = copy

    def arrive(key):
        landed[key].wait_recv()

    def rows_of(p, part):
        first, count = PIECES[p]
        if part is None:
            return (first, count)
        cut = HALF[p]
        return (first, cut) if part == 0 else (first + cut, count - cut)

    def spot(p, ka, kb, kc):
        where = [None] * 3
        for axis, k in ((p, ka), ((p + 1) % 3, kb), ((p + 2) % 3, kc)):
            where[axis] = pl.ds(0, 4) if k is None else (coords[axis] + STEP[k]) % 4
        return where

    def send(key, p, axis, sign, where, rows, from_panel=False):
        src = panel_ref.at[pl.ds(rows[0], rows[1])] if from_panel else view(where, rows)
        push(key, src, view(where, rows), device(shifted(axis, sign), core))

    def twin(key, p, where, rows):
        push(key, view(where, rows), view(where, rows), sibling)

    PS = range(3)
    for p in PS:
        for k, sign in ((1, 1), (2, 3)):
            send((p, 1, k), p, p, sign, spot(p, 0, 0, 0), rows_of(p, None), True)
    for p in PS:
        for k, sign in ((1, 1), (2, 3)):
            send((p, 2, 0, k), p, (p + 1) % 3, sign, spot(p, 0, 0, 0), rows_of(p, None), True)

    lane = lax.broadcasted_iota(jnp.int32, (8, 128), 1)
    table = jnp.zeros((8, 128), jnp.int32)
    for r in range(2):
        def mark(s, found, r=r):
            column = cols_ref[r, s]
            holder = jnp.where(s < counts_ref[r], column >> 1, -1)
            return jnp.where(lane == holder, 1 + 2 * (r * 48 + s) + (column & 1), found)
        table = lax.fori_loop(0, 48, mark, table)
    table_v[...] = table
    table_copy = pltpu.make_async_copy(table_v, table_s, local_sem.at[2])
    table_copy.start()
    sample_ref[...] = jnp.zeros((512, 256), jnp.float32)

    for ka, sign, part in ((1, 1, 0), (2, 3, 1)):
        for p in PS:
            arrive((p, 1, ka))
            send((p, 1, 3, part), p, p, sign, spot(p, ka, 0, 0), rows_of(p, part))
            for k, s in ((1, 1), (2, 3)):
                send((p, 2, ka, k), p, (p + 1) % 3, s, spot(p, ka, 0, 0), rows_of(p, None))
    own.wait()
    table_copy.wait()

    def forward_b(ka):
        for kb, sign, part in ((1, 1, 0), (2, 3, 1)):
            for p in PS:
                arrive((p, 2, ka, kb))
                send((p, 2, ka, 3, part), p, (p + 1) % 3, sign, spot(p, ka, kb, 0), rows_of(p, part))

    def send_c(kb):
        for p in PS:
            for k, s in ((1, 1), (2, 3)):
                send((p, 3, kb, k), p, (p + 2) % 3, s, spot(p, None, kb, 0), rows_of(p, None))
        for p in PS:
            twin((p, 4, kb, 0), p, spot(p, None, kb, 0), rows_of(p, None))

    def forward_c(kb):
        for kc, sign, part in ((1, 1, 0), (2, 3, 1)):
            for p in PS:
                arrive((p, 3, kb, kc))
                send((p, 3, kb, 3, part), p, (p + 2) % 3, sign, spot(p, None, kb, kc), rows_of(p, part))
                twin((p, 4, kb, kc), p, spot(p, None, kb, kc), rows_of(p, None))

    def last_c(kb):
        for p in PS:
            arrive((p, 3, kb, 3, 0))
            arrive((p, 3, kb, 3, 1))
            twin((p, 4, kb, 3), p, spot(p, None, kb, 3), rows_of(p, None))

    def twins(pairs):
        for kb, kc in pairs:
            for p in PS:
                arrive((p, 4, kb, kc))

    def add_products(units):
        tops, bottoms, rights = [], [], []
        for shift, which in units:
            at = [(coords[i] + shift[i]) % 4 for i in range(3)]
            code = table_s[0, device(at, which)]
            index = jnp.maximum(code - 1, 0)
            slot = index >> 1
            block = held[jnp.where(slot >= 48, 1, 0), jnp.where(slot >= 48, slot - 48, slot)]
            none = jnp.zeros_like(block)
            tops.append(jnp.where((code > 0) & (slot < 48), block, none))
            bottoms.append(jnp.where((code > 0) & (slot >= 48), block, none))
            here = panels.at[at[0], at[1], at[2], which]
            rights.append(jnp.where((index & 1) == 0, here[:256], here[256:]))
        left = jnp.concatenate([jnp.concatenate(tops, axis=1), jnp.concatenate(bottoms, axis=1)], axis=0)
        sample_ref[...] += jnp.dot(left, jnp.concatenate(rights, axis=0), preferred_element_type=jnp.float32)

    def near(first, last):
        @pl.loop(first, last)
        def _(i):
            add_products([((i // 3 + 3, i % 3 + 3, k), w) for k in (3, 0, 1) for w in (0, 1)])

    def one_far(first, last):
        @pl.loop(first, last)
        def _(i):
            axis, u = i // 3, i % 3 + 3
            units = []
            for k in (3, 0, 1):
                shift = (jnp.where(axis == 0, 2, k), jnp.where(axis == 1, 2, jnp.where(axis == 0, k, u)), jnp.where(axis == 2, 2, u))
                units += [(shift, 0), (shift, 1)]
            add_products(units)

    def more_far():
        @pl.loop(0, 5)
        def _(i):
            units = []
            for j in (2 * i, 2 * i + 1):
                axis, u = j // 3, j % 3 + 3
                shift = tuple(jnp.where(axis == a, u, 2) for a in range(3))
                units += [(shift, 0), (shift, 1)]
            add_products(units)

    forward_b(0)
    for p in PS:
        arrive((p, 1, 3, 0))
        arrive((p, 1, 3, 1))
        for k, s in ((1, 1), (2, 3)):
            send((p, 2, 3, k), p, (p + 1) % 3, s, spot(p, 3, 0, 0), rows_of(p, None))
    send_c(0)
    forward_b(1)
    forward_b(2)
    forward_b(3)
    send_c(1)
    send_c(2)
    for p in PS:
        for ka in range(4):
            arrive((p, 2, ka, 3, 0))
            arrive((p, 2, ka, 3, 1))
    send_c(3)
    blocks_copy.wait()
    forward_c(0)
    forward_c(1)
    forward_c(2)
    twins([(kb, kc) for kb in range(3) for kc in range(3)])
    near(0, 6)
    forward_c(3)
    near(6, 9)
    last_c(0)
    last_c(1)
    last_c(2)
    twins([(3, kc) for kc in range(3)] + [(kb, 3) for kb in range(3)])
    one_far(0, 9)
    last_c(3)
    twins([(3, 3)])
    more_far()

    v = sample_ref[...]
    gram = lax.dot_general(v, v, (((0,), (0,)), ((), ())), precision=HI, preferred_element_type=jnp.float32)
    local[:128] = gram[:128, :128]
    local[128:256] = gram[:128, 128:]
    local[256:] = gram[128:, 128:]

    def half(which):
        return pl.ds(pl.multiple_of(which * 192, 64), 192)
    pair = pltpu.make_async_remote_copy(
        src_ref=local.at[half(1 - core)], dst_ref=twin_half, send_sem=pair_send.at[0], recv_sem=pair_recv.at[0],
        device_id=(sibling,), device_id_type=MESH)
    pair.start()
    pair.wait_recv()
    both = local[half(core)] + twin_half[...]
    parts = [both[64 * q:64 * q + 64] for q in PS]
    lines = []
    for t in range(3):
        here = []
        for q in PS:
            axis = (q + t) % 3
            mine = terms.at[t, q, coords[axis]]
            mine[...] = parts[q]
            for i in (2, 1, 3):
                copy = pltpu.make_async_remote_copy(
                    src_ref=mine, dst_ref=mine, send_sem=line_send.at[t, q, i - 1], recv_sem=line_recv.at[t, q, i - 1],
                    device_id=(device(shifted(axis, i), core),), device_id_type=MESH)
                copy.start()
                here.append(copy)
        for copy in here:
            copy.wait_recv()
        lines += here
        parts = [(terms[t, q, 0] + terms[t, q, 1]) + (terms[t, q, 2] + terms[t, q, 3]) for q in PS]
    for q in PS:
        gram_ref[pl.ds(pl.multiple_of(core * 192 + 64 * q, 64), 64)] = parts[q]
    back = pltpu.make_async_remote_copy(
        src_ref=gram_ref.at[half(core)], dst_ref=gram_ref.at[half(core)], send_sem=pair_send.at[1], recv_sem=pair_recv.at[1],
        device_id=(sibling,), device_id_type=MESH)
    back.start()
    back.wait_recv()
    for copy in started + lines + [pair, back]:
        copy.wait_send()
    assert len(started) == N_COPIES


def sample_and_gram(cols, counts, blocks, panel):
    return pl.pallas_call(
        sample_kernel,
        out_shape=(jax.ShapeDtypeStruct((512, 256), jnp.float32), jax.ShapeDtypeStruct((384, 128), jnp.float32)),
        in_specs=[pl.BlockSpec(memory_space=pltpu.SMEM)] * 2 + [pl.BlockSpec(memory_space=pl.ANY)] * 2,
        out_specs=(pl.BlockSpec(memory_space=pltpu.VMEM),) * 2,
        scratch_shapes=[
            pltpu.VMEM((4, 4, 4, 2, 512, 256), jnp.bfloat16),
            pltpu.VMEM((2, 48, 256, 256), jnp.bfloat16),
            pltpu.VMEM((8, 128), jnp.int32),
            pltpu.SMEM((8, 128), jnp.int32),
            pltpu.VMEM((384, 128), jnp.float32),
            pltpu.VMEM((192, 128), jnp.float32),
            pltpu.VMEM((3, 3, 4, 64, 128), jnp.float32),
            pltpu.SemaphoreType.DMA((N_COPIES,)),
            pltpu.SemaphoreType.DMA((N_COPIES,)),
            pltpu.SemaphoreType.DMA((3,)),
            pltpu.SemaphoreType.DMA((3, 3, 3)),
            pltpu.SemaphoreType.DMA((3, 3, 3)),
            pltpu.SemaphoreType.DMA((2,)),
            pltpu.SemaphoreType.DMA((2,)),
        ],
        compiler_params=pltpu.CompilerParams(collective_id=0, has_side_effects=True, vmem_limit_bytes=56 << 20),
        name="sample_gram",
    )(cols, counts, blocks, panel)


def dot(a, b, ca=1, cb=0):
    return lax.dot_general(a, b, (((ca,), (cb,)), ((), ())), precision=HI, preferred_element_type=jnp.float32)

def recip(x):
    r = pl.reciprocal(x, approx=True)
    return r * (2.0 - x * r)

def eliminate2(s, n=128):
    g = n // 8
    sub = lax.broadcasted_iota(jnp.int32, (8, n), 0)
    lane = lax.broadcasted_iota(jnp.int32, (8, n), 1)
    S = [s[8*i:8*i+8] for i in range(g)]
    W = [jnp.where(lane == sub + 8*i, 1.0, 0.0).astype(jnp.float32) for i in range(g)]
    for j in range(0, n, 2):
        k, r = divmod(j, 8)
        b0 = [None]*k + [jnp.broadcast_to(S[i][:, j:j+1], (8, n)) for i in range(k, g)]
        b1 = [None]*k + [jnp.broadcast_to(S[i][:, j+1:j+2], (8, n)) for i in range(k, g)]
        def row(x, q): return jnp.broadcast_to(x[q:q+1], (8, n))
        a = row(b0[k], r); b = row(b0[k], r+1); c = row(b1[k], r+1)
        s0 = row(S[k], r); s1 = row(S[k], r+1); w0 = row(W[k], r); w1 = row(W[k], r+1)
        idet = recip(a*c - b*b)
        t0 = (c*s0 - b*s1)*idet; t1 = (a*s1 - b*s0)*idet
        u0 = (c*w0 - b*w1)*idet; u1 = (a*w1 - b*w0)*idet
        ia = recip(a)
        l = b*ia
        for i in range(k, g):
            if i == k:
                m0 = jnp.where(sub > r+1, b0[i], 0.0); m1 = jnp.where(sub > r+1, b1[i], 0.0)
                ns = S[i] - m0*t0 - m1*t1
                nw = W[i] - m0*u0 - m1*u1
                S[i] = jnp.where(sub == r+1, ns - l*s0, ns)
                W[i] = jnp.where(sub == r+1, nw - l*w0, nw)
            else:
                S[i] = S[i] - b0[i]*t0 - b1[i]*t1
                W[i] = W[i] - b0[i]*u0 - b1[i]*u1
    return S, W

def finish(S, W, n=128):
    g = n // 8
    sub = lax.broadcasted_iota(jnp.int32, (8, n), 0)
    lane = lax.broadcasted_iota(jnp.int32, (8, n), 1)
    R, V = [], []
    for i in range(g):
        d = jnp.sum(jnp.where(lane == sub + 8*i, S[i], 0.0), axis=1, keepdims=True)
        q = lax.rsqrt(d)
        q = q*(1.5 - 0.5*d*q*q)
        R.append(jnp.where(lane >= sub + 8*i, S[i]*q, 0.0))
        V.append(W[i]*q)
    return jnp.concatenate(R, 0), jnp.concatenate(V, 0)

def factor(gram_ref, elim):
    R11, V11 = finish(*elim(gram_ref[:128]))
    R12 = dot(V11, gram_ref[128:256])
    s = gram_ref[256:] - dot(R12, R12, 0, 0)
    R22, V22 = finish(*elim(s))
    V21 = -dot(V22, dot(R12, V11, 0, 0))
    return R11, R12, R22, V11, V21, V22

def chol_kernel(elim, gram_ref, sample_ref, basis_ref, tri_ref):
    R11, R12, R22, V11, V21, V22 = factor(gram_ref, elim)
    sc = 1.0/256
    tri_ref[:128, :128] = R11*sc
    tri_ref[:128, 128:] = R12*sc
    tri_ref[128:, :128] = jnp.zeros((128, 128), jnp.float32)
    tri_ref[128:, 128:] = R22*sc
    s1 = sample_ref[:, :128]; s2 = sample_ref[:, 128:]
    basis_ref[:, :128] = dot(s1, V11*256.0, 1, 1)
    basis_ref[:, 128:] = dot(s1, V21*256.0, 1, 1) + dot(s2, V22*256.0, 1, 1)

def chol(gram, sample, elim=eliminate2):
    return pl.pallas_call(functools.partial(chol_kernel, elim),
        out_shape=(jax.ShapeDtypeStruct(sample.shape, jnp.float32), jax.ShapeDtypeStruct((256,256), jnp.float32)),
        in_specs=[pl.BlockSpec(memory_space=pltpu.VMEM)]*2, out_specs=(pl.BlockSpec(memory_space=pltpu.VMEM),)*2,
        compiler_params=pltpu.CompilerParams(vmem_limit_bytes=32<<20), name="chol")(gram, sample)


def per_device(matrix_blocks, test_panel, column_blocks, row_counts):
    values, gram = sample_and_gram(column_blocks, row_counts, matrix_blocks, test_panel)
    return chol(gram, values)


def solution(mesh):
    in_specs = (P("row", None, None, None), P("row", None), P("row", None), P("row"))
    return jax.shard_map(
        per_device, mesh=mesh, in_specs=in_specs, out_specs=(P("row", None), P()), check_vma=False
    )
```

time: 1040 us -> 126 us (0.12)
  waiting for transfers between devices: 375 us -> 0 us
  loops' own time: 198 us -> 0 us
  local copies, waits for them, and re-layouts: 191 us -> 1.96 us
  matrix products: 133 us -> 0 us
  Pallas kernels: 0 us -> 124 us
  other arithmetic: 99 us -> 0 us
  blocking collectives: 20.7 us -> 0 us
  between operations: 14.1 us -> 0.65 us
    all_to_all x1 -> x0, waiting for transfers between devices: 220 us -> none  [per_device(): lax.all_to_all(reply, 'row', split_axis=0, concat_axis=0, tiled=True)]
    another operation x1 -> x0, loops' own time: 198 us -> none  [factor_pair(): lower, inverse = lax.fori_loop(0, order, column_step, (start, start))]
    dynamic_slice x512 -> x0, local copies, waits for them, and re-layouts: 167 us -> none  [the longest x256 151 us: column_step(): pivot = jnp.sqrt(lax.dynamic_slice_in_dim(current, column, 1, 0)[0])]
    psum x1 -> x0, waiting for transfers between devices: 154 us -> none  [per_device(): gram = lax.psum(jnp.dot(sample.T, sample, precision=highest), 'row')]
    dot_general x515 -> x0, matrix products: 133 us -> none  [the longest x256 67.9 us: column_step(): jnp.dot(lower, row_now, precision=highest)]
    pallas_call x0 -> x2, Pallas kernels: none -> 124 us  [the longest x1 102 us: sample_and_gram(): pl.pallas_call(sample_kernel, out_shape=(jax.ShapeDtypeStruct((512, 256),...]
    add x512 -> x0, other arithmetic: 58.2 us -> none  [the longest x256 29.6 us: column_step(): inverse = inverse + pick[:, None] * inverse_row[None, :]]
    all_to_all x1 -> x0, blocking collectives: 20.7 us -> none  [per_device(): lax.all_to_all(wanted.reshape(devices, capacity), 'row', split_axis=0, co...]
  transfers between devices with their start and end apart: 2 -> 0, of which waited for: 2 -> 0; matrix products, arithmetic and copies ran while one was open for 0% -> 0% of each run, Pallas kernels for 0% -> 0%
where the time goes in v1:
time: 126 us
  Pallas kernels  124 us (98%)
  local copies, waits for them, and re-layouts  1.96 us (2%)
    pallas_call x1, Pallas kernels, sample_and_gram(): pl.pallas_call(sample_kernel, out_shape=(jax.ShapeDtypeStruct((512, 256),...  102 us
    pallas_call x1, Pallas kernels, chol(): pl.pallas_call(functools.partial(chol_kernel, elim), out_shape=(jax.Shape...  21.3 us

profile of v1, /device:TPU:1, one launch (start us, length us, event | category | flops | bytes accessed | tf_op | source)
XLA Modules:
  0.0 126.3 jit_solution(13352083604914677258)
XLA Ops:
  0.6 102.3 %sample_gram.1 = (f32[512,256]{1,0:T(8,128)}, f32[384,128]{1,0:T(8,128)}) custom-call(s32[2,48]{1,0:T(2,128)} %cols_ref.1, s32[2]{0:T(128)} %counts_ref.1, bf16[2,48,256,256]{3,2,1,0:T(8,128)(2,1)} %blocks_ref.1, bf16[512,256]{1,0:T(8,128)(2,1)} %panel_ref.1), custom_call_target="tpu_custom_call" | custom-call | tf_op jit(solution)/shard_map/sample_gram/pallas_call | solution.py:264
  103.0 0.0 copy-start
  103.0 1.0 copy-done
  104.0 0.0 copy-start.1
  104.0 0.9 copy-done.1
  105.0 21.3 %chol.1 = (f32[512,256]{1,0:T(8,128)}, f32[256,256]{1,0:T(8,128)}) custom-call(f32[384,128]{1,0:T(8,128)S(1)} %copy-done.1, f32[512,256]{1,0:T(8,128)S(1)} %copy-done), custom_call_target="tpu_custom_call" | custom-call | tf_op jit(solution)/shard_map/chol/pallas_call | solution.py:360
Async XLA Ops:
  103.0 1.0 copy-start
  104.0 0.9 copy-start.1

commit v2 on v1

v2 whole, which is shorter than its diff:
```python
import functools

import jax
import jax.numpy as jnp
from jax import lax
from jax.experimental import pallas as pl
from jax.experimental.pallas import tpu as pltpu
from jax.sharding import PartitionSpec as P

MESH = pl.DeviceIdType.MESH
HI = lax.Precision.HIGHEST


PIECES = ((0, 176), (176, 176), (352, 160))
HALF = (96, 80, 80)
STEP = (0, 3, 1, 2)
N_COPIES = 180


def sample_kernel(cols_ref, counts_ref, blocks_ref, panel_ref, sample_out, gram_ref, panels, held, sample_ref, table_v, table_s, local, twin_half, terms, send_sem, recv_sem, local_sem, line_send, line_recv, pair_send, pair_recv):
    me = lax.axis_index("row")
    core = me % 2
    coords = [me // 32, (me // 8) % 4, (me // 2) % 4]

    def device(at, which):
        return at[0] * 32 + at[1] * 8 + at[2] * 2 + which

    def shifted(axis, by):
        at = list(coords)
        at[axis] = (at[axis] + by) % 4
        return at

    sibling = device(coords, 1 - core)
    partners = [device(shifted(a, s), core) for a in range(3) for s in (1, 2, 3)] + [sibling]
    barrier = pltpu.get_barrier_semaphore()
    for other in partners:
        pl.semaphore_signal(barrier, inc=1, device_id=(other,), device_id_type=MESH)
    blocks_copy = pltpu.make_async_copy(blocks_ref, held, local_sem.at[0])
    blocks_copy.start()
    own = pltpu.make_async_copy(panel_ref, panels.at[coords[0], coords[1], coords[2], core], local_sem.at[1])
    own.start()
    pl.semaphore_wait(barrier, len(partners))

    started = []
    landed = {}

    def view(where, rows, which=core):
        return panels.at[where[0], where[1], where[2], which, pl.ds(rows[0], rows[1])]

    def push(key, src, dst, target):
        slot = len(started)
        copy = pltpu.make_async_remote_copy(
            src_ref=src, dst_ref=dst, send_sem=send_sem.at[slot], recv_sem=recv_sem.at[slot],
            device_id=(target,), device_id_type=MESH)
        copy.start()
        started.append(copy)
        landed[key] = copy

    def arrive(key):
        landed[key].wait_recv()

    def rows_of(p, part, flip=0):
        first, count = PIECES[p]
        if part is None:
            return (first, count)
        cut = count - HALF[p] if flip else HALF[p]
        return (first, cut) if part == 0 else (first + cut, count - cut)

    def spot(p, ka, kb, kc, among=(0, 4)):
        where = [None] * 3
        for axis, k in ((p, ka), ((p + 1) % 3, kb), ((p + 2) % 3, kc)):
            where[axis] = pl.ds(*among) if k is None else (coords[axis] + STEP[k]) % 4
        return where

    def send(key, p, axis, sign, where, rows, from_panel=False):
        src = panel_ref.at[pl.ds(rows[0], rows[1])] if from_panel else view(where, rows)
        push(key, src, view(where, rows), device(shifted(axis, sign), core))

    def twin(key, p, where, rows):
        push(key, view(where, rows), view(where, rows), sibling)

    PS = range(3)
    for p in PS:
        for k, sign in ((1, 1), (2, 3)):
            send((p, 1, k), p, p, sign, spot(p, 0, 0, 0), rows_of(p, None), True)
    for p in PS:
        for k, sign in ((1, 1), (2, 3)):
            send((p, 2, 0, k), p, (p + 1) % 3, sign, spot(p, 0, 0, 0), rows_of(p, None), True)

    lane = lax.broadcasted_iota(jnp.int32, (8, 128), 1)
    table = jnp.zeros((8, 128), jnp.int32)
    for r in range(2):
        def mark(s, found, r=r):
            column = cols_ref[r, s]
            holder = jnp.where(s < counts_ref[r], column >> 1, -1)
            return jnp.where(lane == holder, 1 + 2 * (r * 48 + s) + (column & 1), found)
        table = lax.fori_loop(0, 48, mark, table)
    table_v[...] = table
    table_copy = pltpu.make_async_copy(table_v, table_s, local_sem.at[2])
    table_copy.start()
    sample_ref[...] = jnp.zeros((512, 256), jnp.float32)

    for ka, sign, part in ((1, 1, 0), (2, 3, 1)):
        for p in PS:
            arrive((p, 1, ka))
            send((p, 1, 3, part), p, p, sign, spot(p, ka, 0, 0), rows_of(p, part, p % 2))
            for k, s in ((1, 1), (2, 3)):
                send((p, 2, ka, k), p, (p + 1) % 3, s, spot(p, ka, 0, 0), rows_of(p, None))
    own.wait()
    table_copy.wait()

    def forward_b(ka):
        for kb, sign, part in ((1, 1, 0), (2, 3, 1)):
            for p in PS:
                arrive((p, 2, ka, kb))
                send((p, 2, ka, 3, part), p, (p + 1) % 3, sign, spot(p, ka, kb, 0), rows_of(p, part, ka % 2))

    def send_c(kb):
        for p in PS:
            for k, s in ((1, 1), (2, 3)):
                send((p, 3, kb, k), p, (p + 2) % 3, s, spot(p, None, kb, 0), rows_of(p, None))
        for p in PS:
            twin((p, 4, kb, 0), p, spot(p, None, kb, 0), rows_of(p, None))

    def cuts(kb):
        return ((0, 2), (2, 2)) if kb == 3 else ((0, 4),)

    def forward_c(kb):
        for kc, sign, part in ((1, 1, 0), (2, 3, 1)):
            for p in PS:
                arrive((p, 3, kb, kc))
                for among in cuts(kb):
                    send((p, 3, kb, 3, part, among), p, (p + 2) % 3, sign, spot(p, None, kb, kc, among), rows_of(p, part, kb % 2))
                twin((p, 4, kb, kc), p, spot(p, None, kb, kc), rows_of(p, None))

    def last_c(kb):
        for among in cuts(kb):
            for p in PS:
                for part in range(2):
                    arrive((p, 3, kb, 3, part, among))
                    twin((p, 4, kb, 3, part, among), p, spot(p, None, kb, 3, among), rows_of(p, part, kb % 2))

    def twins(pairs):
        for kb, kc in pairs:
            for p in PS:
                if kc < 3:
                    arrive((p, 4, kb, kc))
                    continue
                for among in cuts(kb):
                    for part in range(2):
                        arrive((p, 4, kb, 3, part, among))

    def add_products(units):
        tops, bottoms, rights = [], [], []
        for shift, which in units:
            at = [(coords[i] + shift[i]) % 4 for i in range(3)]
            code = table_s[0, device(at, which)]
            index = jnp.maximum(code - 1, 0)
            slot = index >> 1
            block = held[jnp.where(slot >= 48, 1, 0), jnp.where(slot >= 48, slot - 48, slot)]
            none = jnp.zeros_like(block)
            tops.append(jnp.where((code > 0) & (slot < 48), block, none))
            bottoms.append(jnp.where((code > 0) & (slot >= 48), block, none))
            here = panels.at[at[0], at[1], at[2], which]
            rights.append(jnp.where((index & 1) == 0, here[:256], here[256:]))
        left = jnp.concatenate([jnp.concatenate(tops, axis=1), jnp.concatenate(bottoms, axis=1)], axis=0)
        sample_ref[...] += jnp.dot(left, jnp.concatenate(rights, axis=0), preferred_element_type=jnp.float32)

    def near(first, last):
        @pl.loop(first, last)
        def _(i):
            add_products([((i // 3 + 3, i % 3 + 3, k), w) for k in (3, 0, 1) for w in (0, 1)])

    def one_far(kb, which):
        @pl.loop(0, 3)
        def _(i):
            add_products([
                (tuple(jnp.where(axis == i, 2, jnp.where(axis == (i + 2) % 3, STEP[kb], k)) for axis in range(3)), which)
                for k in (3, 0, 1)])

    def more_far(which):
        @pl.loop(0, 2)
        def _(i):
            units = []
            for n in range(5):
                j = 5 * i + n
                axis, u = j // 3, j % 3 + 3
                units.append((tuple(jnp.where(axis == a, u, 2) for a in range(3)), which))
            add_products(units)

    forward_b(0)
    for p in PS:
        arrive((p, 1, 3, 0))
        arrive((p, 1, 3, 1))
        for k, s in ((1, 1), (2, 3)):
            send((p, 2, 3, k), p, (p + 1) % 3, s, spot(p, 3, 0, 0), rows_of(p, None))
    send_c(0)
    forward_b(1)
    forward_b(2)
    forward_b(3)
    send_c(1)
    send_c(2)
    for p in PS:
        for ka in range(4):
            arrive((p, 2, ka, 3, 0))
            arrive((p, 2, ka, 3, 1))
    send_c(3)
    blocks_copy.wait()
    forward_c(0)
    forward_c(1)
    forward_c(2)
    twins([(kb, kc) for kb in range(3) for kc in range(3)])
    near(0, 6)
    forward_c(3)
    near(6, 9)
    last_c(0)
    one_far(0, core)
    last_c(1)
    twins([(3, kc) for kc in range(3)] + [(0, 3)])
    one_far(0, 1 - core)
    one_far(1, core)
    last_c(2)
    twins([(1, 3)])
    one_far(1, 1 - core)
    one_far(2, core)
    last_c(3)
    twins([(2, 3)])
    one_far(2, 1 - core)
    more_far(core)
    twins([(3, 3)])
    more_far(1 - core)

    sample_copy = pltpu.make_async_copy(sample_ref, sample_out, local_sem.at[3])
    sample_copy.start()
    v = sample_ref[...]
    gram = lax.dot_general(v, v, (((0,), (0,)), ((), ())), precision=HI, preferred_element_type=jnp.float32)
    local[:128] = gram[:128, :128]
    local[128:256] = gram[:128, 128:]
    local[256:] = gram[128:, 128:]

    def part_rows(which, q):
        return pl.ds(pl.multiple_of(which * 192 + 64 * q, 64), 64)

    pairs, lines, backs = [], {}, []
    for q in PS:
        pairs.append(pltpu.make_async_remote_copy(
            src_ref=local.at[part_rows(1 - core, q)], dst_ref=twin_half.at[q], send_sem=pair_send.at[0, q], recv_sem=pair_recv.at[0, q],
            device_id=(sibling,), device_id_type=MESH))
        pairs[q].start()

    def along(t, q, value):
        axis = (q + t) % 3
        mine = terms.at[t, q, coords[axis]]
        mine[...] = value
        for i in (2, 1, 3):
            copy = pltpu.make_async_remote_copy(
                src_ref=mine, dst_ref=mine, send_sem=line_send.at[t, q, i - 1], recv_sem=line_recv.at[t, q, i - 1],
                device_id=(device(shifted(axis, i), core),), device_id_type=MESH)
            copy.start()
            lines[t, q, i] = copy

    for q in PS:
        pairs[q].wait_recv()
        along(0, q, local[part_rows(core, q)] + twin_half[q])
    for t in range(3):
        for q in PS:
            for i in (1, 3, 2):
                lines[t, q, i].wait_recv()
            total = (terms[t, q, 0] + terms[t, q, 1]) + (terms[t, q, 2] + terms[t, q, 3])
            if t < 2:
                along(t + 1, q, total)
                continue
            gram_ref[part_rows(core, q)] = total
            backs.append(pltpu.make_async_remote_copy(
                src_ref=gram_ref.at[part_rows(core, q)], dst_ref=gram_ref.at[part_rows(core, q)], send_sem=pair_send.at[1, q], recv_sem=pair_recv.at[1, q],
                device_id=(sibling,), device_id_type=MESH))
            backs[q].start()
    for copy in backs:
        copy.wait_recv()
    for copy in started + list(lines.values()) + pairs + backs:
        copy.wait_send()
    sample_copy.wait()
    assert len(started) == N_COPIES, len(started)


def sample_and_gram(cols, counts, blocks, panel):
    return pl.pallas_call(
        sample_kernel,
        out_shape=(jax.ShapeDtypeStruct((512, 256), jnp.float32), jax.ShapeDtypeStruct((384, 128), jnp.float32)),
        in_specs=[pl.BlockSpec(memory_space=pltpu.SMEM)] * 2 + [pl.BlockSpec(memory_space=pl.ANY)] * 2,
        out_specs=(pl.BlockSpec(memory_space=pl.ANY), pl.BlockSpec(memory_space=pltpu.VMEM)),
        scratch_shapes=[
            pltpu.VMEM((4, 4, 4, 2, 512, 256), jnp.bfloat16),
            pltpu.VMEM((2, 48, 256, 256), jnp.bfloat16),
            pltpu.VMEM((512, 256), jnp.float32),
            pltpu.VMEM((8, 128), jnp.int32),
            pltpu.SMEM((8, 128), jnp.int32),
            pltpu.VMEM((384, 128), jnp.float32),
            pltpu.VMEM((3, 64, 128), jnp.float32),
            pltpu.VMEM((3, 3, 4, 64, 128), jnp.float32),
            pltpu.SemaphoreType.DMA((N_COPIES,)),
            pltpu.SemaphoreType.DMA((N_COPIES,)),
            pltpu.SemaphoreType.DMA((4,)),
            pltpu.SemaphoreType.DMA((3, 3, 3)),
            pltpu.SemaphoreType.DMA((3, 3, 3)),
            pltpu.SemaphoreType.DMA((2, 3)),
            pltpu.SemaphoreType.DMA((2, 3)),
        ],
        compiler_params=pltpu.CompilerParams(collective_id=0, has_side_effects=True, vmem_limit_bytes=56 << 20),
        name="sample_gram",
    )(cols, counts, blocks, panel)


def dot(a, b, ca=1, cb=0):
    return lax.dot_general(a, b, (((ca,), (cb,)), ((), ())), precision=HI, preferred_element_type=jnp.float32)


def reciprocal(x):
    r = pl.reciprocal(x, approx=True)
    return r * (2.0 - x * r)


def factor_half(s, n=128):
    tiles = n // 8
    sub = lax.broadcasted_iota(jnp.int32, (8, n), 0)
    lane = lax.broadcasted_iota(jnp.int32, (8, n), 1)
    S = [s[8 * i:8 * i + 8] for i in range(tiles)]
    W = [jnp.where(lane == sub + 8 * i, 1.0, 0.0).astype(jnp.float32) for i in range(tiles)]

    def row(x, i):
        return jnp.broadcast_to(x[i:i + 1], (8, n))

    def column(x, j):
        return jnp.broadcast_to(x[:, j:j + 1], (8, n))

    for k in range(tiles):
        cols = [column(S[k], 8 * k + j) for j in range(8)]
        e = {(i, j): row(cols[j], i) for j in range(8) for i in range(j + 1)}
        r = [row(S[k], i) for i in range(8)]
        w = [row(W[k], i) for i in range(8)]
        inv, g, ahead = {}, {}, {}
        follow = k + 1 < tiles
        side = [column(S[k + 1], 8 * k + q) for q in range(8)] if follow else None
        kept = list(side) if follow else None
        for j in range(0, 8, 2):
            a, b, c = e[j, j], e[j, j + 1], e[j + 1, j + 1]
            det = a * c - b * b
            rough = pl.reciprocal(det, approx=True)
            near = 2.0 - det * rough
            inv[j] = rough * near
            ahead[j] = c * r[j] - b * r[j + 1], a * r[j + 1] - b * r[j], c * w[j] - b * w[j + 1], a * w[j + 1] - b * w[j]
            if follow:
                S[k + 1] = S[k + 1] - ((side[j] * ahead[j][0] + side[j + 1] * ahead[j][1]) * rough) * near
            for i in range(j + 2, 8):
                x, y = e[j, i], e[j + 1, i]
                n0, n1 = c * x - b * y, a * y - b * x
                for q in range(i, 8):
                    e[i, q] = e[i, q] - ((n0 * e[j, q] + n1 * e[j + 1, q]) * rough) * near
                g[i, j], g[i, j + 1] = n0 * inv[j], n1 * inv[j]
                if follow:
                    side[i] = side[i] - (g[i, j] * side[j] + g[i, j + 1] * side[j + 1])
                r[i] = r[i] - (g[i, j] * r[j] + g[i, j + 1] * r[j + 1])
                w[i] = w[i] - (g[i, j] * w[j] + g[i, j + 1] * w[j + 1])
        if k + 1 < tiles:
            t, u = [None] * 8, [None] * 8
            for j in (6, 4, 2, 0):
                t[j], t[j + 1], u[j], u[j + 1] = [v * inv[j] for v in ahead[j]]
                for m in range(j + 2, 8, 2):
                    for h in (j, j + 1):
                        t[h] = t[h] - (g[m, h] * t[m] + g[m + 1, h] * t[m + 1])
                        u[h] = u[h] - (g[m, h] * u[m] + g[m + 1, h] * u[m + 1])
            for i in range(k + 1, tiles):
                c = kept if i == k + 1 else [column(S[i], 8 * k + q) for q in range(8)]
                S[i] = S[i] if i == k + 1 else ((S[i] - (c[6] * t[6] + c[7] * t[7])) - (c[4] * t[4] + c[5] * t[5])) - (c[2] * t[2] + c[3] * t[3]) - (c[0] * t[0] + c[1] * t[1])
                W[i] = ((W[i] - (c[6] * u[6] + c[7] * u[7])) - (c[4] * u[4] + c[5] * u[5])) - (c[2] * u[2] + c[3] * u[3]) - (c[0] * u[0] + c[1] * u[1])
        for j in range(0, 8, 2):
            slope = e[j, j + 1] * reciprocal(e[j, j])
            r[j + 1] = r[j + 1] - slope * r[j]
            w[j + 1] = w[j + 1] - slope * w[j]
            e[j + 1, j + 1] = e[j + 1, j + 1] - slope * e[j, j + 1]
        new_s, new_w = r[0], w[0]
        d = e[0, 0]
        for i in range(1, 8):
            new_s = jnp.where(sub == i, r[i], new_s)
            new_w = jnp.where(sub == i, w[i], new_w)
            d = jnp.where(sub == i, e[i, i], d)
        q = lax.rsqrt(d)
        q = q * (1.5 - 0.5 * d * q * q)
        S[k] = jnp.where(lane >= sub + 8 * k, new_s * q, 0.0)
        W[k] = new_w * q
    return jnp.concatenate(S, axis=0), jnp.concatenate(W, axis=0)


def chol_kernel(gram_hbm, sample_hbm, basis_ref, tri_ref, gram_ref, sample_ref, sems):
    gram_copy = pltpu.make_async_copy(gram_hbm, gram_ref, sems.at[0])
    sample_copy = pltpu.make_async_copy(sample_hbm, sample_ref, sems.at[1])
    gram_copy.start()
    sample_copy.start()
    gram_copy.wait()
    R11, V11 = factor_half(gram_ref[:128])
    R12 = dot(V11, gram_ref[128:256])
    rest = gram_ref[256:] - dot(R12, R12, 0, 0)
    scale = 1.0 / 256
    sample_copy.wait()
    first = dot(sample_ref[:, :128], V11 * 256.0, 1, 1)
    second = sample_ref[:, 128:] * 256.0 - dot(first, R12)
    basis_ref[:, :128] = first
    tri_ref[:128, :128] = R11 * scale
    tri_ref[:128, 128:] = R12 * scale
    tri_ref[128:, :128] = jnp.zeros((128, 128), jnp.float32)
    R22, V22 = factor_half(rest)
    tri_ref[128:, 128:] = R22 * scale
    basis_ref[:, 128:] = dot(second, V22, 1, 1)


def chol(gram, values):
    return pl.pallas_call(
        chol_kernel,
        out_shape=(jax.ShapeDtypeStruct((512, 256), jnp.float32), jax.ShapeDtypeStruct((256, 256), jnp.float32)),
        in_specs=[pl.BlockSpec(memory_space=pl.ANY)] * 2,
        out_specs=(pl.BlockSpec(memory_space=pltpu.VMEM),) * 2,
        scratch_shapes=[pltpu.VMEM((384, 128), jnp.float32), pltpu.VMEM((512, 256), jnp.float32), pltpu.SemaphoreType.DMA((2,))],
        compiler_params=pltpu.CompilerParams(vmem_limit_bytes=56 << 20),
        name="factor_basis",
    )(gram, values)


def per_device(matrix_blocks, test_panel, column_blocks, row_counts):
    values, gram = sample_and_gram(column_blocks, row_counts, matrix_blocks, test_panel)
    return chol(gram, values)


def solution(mesh):
    in_specs = (P("row", None, None, None), P("row", None), P("row", None), P("row"))
    return jax.shard_map(
        per_device, mesh=mesh, in_specs=in_specs, out_specs=(P("row", None), P()), check_vma=False
    )
```

time: 126 us -> 108 us (0.86)
  Pallas kernels: 124 us -> 107 us
  local copies, waits for them, and re-layouts: 1.96 us -> 0 us
    pallas_call x1, Pallas kernels: 21.3 us -> 11.3 us  [chol(): pl.pallas_call(chol_kernel, out_shape=(jax.ShapeDtypeStruct((512, 256), j...]
    pallas_call x1, Pallas kernels: 102 us -> 95.9 us  [sample_and_gram(): pl.pallas_call(sample_kernel, out_shape=(jax.ShapeDtypeStruct((512, 256),...]
    unnamed x4 -> x0, local copies, waits for them, and re-layouts: 1.96 us -> none
where the time goes in v2:
time: 108 us
  Pallas kernels  107 us (99%)
    pallas_call x1, Pallas kernels, sample_and_gram(): pl.pallas_call(sample_kernel, out_shape=(jax.ShapeDtypeStruct((512, 256),...  95.9 us
    pallas_call x1, Pallas kernels, chol(): pl.pallas_call(chol_kernel, out_shape=(jax.ShapeDtypeStruct((512, 256), j...  11.3 us

profile of v2, /device:TPU:1, one launch (start us, length us, event | category | flops | bytes accessed | tf_op | source)
XLA Modules:
  0.0 108.0 jit_solution(10769014064680272032)
XLA Ops:
  0.6 95.9 %sample_gram.1 = (f32[512,256]{1,0:T(8,128)}, f32[384,128]{1,0:T(8,128)}) custom-call(s32[2,48]{1,0:T(2,128)} %cols_ref.1, s32[2]{0:T(128)} %counts_ref.1, bf16[2,48,256,256]{3,2,1,0:T(8,128)(2,1)} %blocks_ref.1, bf16[512,256]{1,0:T(8,128)(2,1)} %panel_ref.1), custom_call_target="tpu_custom_call" | custom-call | tf_op jit(solution)/shard_map/sample_gram/pallas_call | solution.py:287
  96.6 11.3 %factor_basis.1 = (f32[512,256]{1,0:T(8,128)}, f32[256,256]{1,0:T(8,128)}) custom-call(f32[384,128]{1,0:T(8,128)} %get-tuple-element.4.gram_hbm, f32[512,256]{1,0:T(8,128)} %get-tuple-element.5.sample_hbm), custom_call_target="tpu_custom_call" | custom-call | tf_op jit(solution)/shard_map/factor_basis/pallas_call | solution.py:417

commit v3 on v2

--- a/solution.py
+++ b/solution.py
@@ -11,8 +11,8 @@
 HI = lax.Precision.HIGHEST
 
 
-PIECES = ((0, 176), (176, 176), (352, 160))
-HALF = (96, 80, 80)
+PIECES = ((0, 160), (160, 176), (336, 176))
+HALF = (80, 96, 80)
 STEP = (0, 3, 1, 2)
 N_COPIES = 180
 
@@ -315,29 +315,31 @@
     return lax.dot_general(a, b, (((ca,), (cb,)), ((), ())), precision=HI, preferred_element_type=jnp.float32)
 
 
-def reciprocal(x):
-    r = pl.reciprocal(x, approx=True)
-    return r * (2.0 - x * r)
-
-
-def factor_half(s, n=128):
+def factor_half(s, spread, n=128):
     tiles = n // 8
     sub = lax.broadcasted_iota(jnp.int32, (8, n), 0)
     lane = lax.broadcasted_iota(jnp.int32, (8, n), 1)
     S = [s[8 * i:8 * i + 8] for i in range(tiles)]
     W = [jnp.where(lane == sub + 8 * i, 1.0, 0.0).astype(jnp.float32) for i in range(tiles)]
 
-    def row(x, i):
-        return jnp.broadcast_to(x[i:i + 1], (8, n))
+    def row(place, i):
+        return spread[pl.ds(8 * place + i, 8, stride=0), :]
+
+    def put(place, x):
+        spread[8 * place:8 * place + 8, :] = x
 
     def column(x, j):
         return jnp.broadcast_to(x[:, j:j + 1], (8, n))
 
     for k in range(tiles):
         cols = [column(S[k], 8 * k + j) for j in range(8)]
-        e = {(i, j): row(cols[j], i) for j in range(8) for i in range(j + 1)}
-        r = [row(S[k], i) for i in range(8)]
-        w = [row(W[k], i) for i in range(8)]
+        for j in range(8):
+            put(10 * k + j, cols[j])
+        put(10 * k + 8, S[k])
+        put(10 * k + 9, W[k])
+        e = {(i, j): row(10 * k + j, i) for j in range(8) for i in range(j + 1)}
+        r = [row(10 * k + 8, i) for i in range(8)]
+        w = [row(10 * k + 9, i) for i in range(8)]
         inv, g, ahead = {}, {}, {}
         follow = k + 1 < tiles
         side = [column(S[k + 1], 8 * k + q) for q in range(8)] if follow else None
@@ -345,17 +347,15 @@
         for j in range(0, 8, 2):
             a, b, c = e[j, j], e[j, j + 1], e[j + 1, j + 1]
             det = a * c - b * b
-            rough = pl.reciprocal(det, approx=True)
-            near = 2.0 - det * rough
-            inv[j] = rough * near
+            inv[j] = pl.reciprocal(det, approx=True)
             ahead[j] = c * r[j] - b * r[j + 1], a * r[j + 1] - b * r[j], c * w[j] - b * w[j + 1], a * w[j + 1] - b * w[j]
             if follow:
-                S[k + 1] = S[k + 1] - ((side[j] * ahead[j][0] + side[j + 1] * ahead[j][1]) * rough) * near
+                S[k + 1] = S[k + 1] - ((side[j] * ahead[j][0] + side[j + 1] * ahead[j][1]) * inv[j])
             for i in range(j + 2, 8):
                 x, y = e[j, i], e[j + 1, i]
                 n0, n1 = c * x - b * y, a * y - b * x
                 for q in range(i, 8):
-                    e[i, q] = e[i, q] - ((n0 * e[j, q] + n1 * e[j + 1, q]) * rough) * near
+                    e[i, q] = e[i, q] - ((n0 * e[j, q] + n1 * e[j + 1, q]) * inv[j])
                 g[i, j], g[i, j + 1] = n0 * inv[j], n1 * inv[j]
                 if follow:
                     side[i] = side[i] - (g[i, j] * side[j] + g[i, j + 1] * side[j + 1])
@@ -374,7 +374,7 @@
                 S[i] = S[i] if i == k + 1 else ((S[i] - (c[6] * t[6] + c[7] * t[7])) - (c[4] * t[4] + c[5] * t[5])) - (c[2] * t[2] + c[3] * t[3]) - (c[0] * t[0] + c[1] * t[1])
                 W[i] = ((W[i] - (c[6] * u[6] + c[7] * u[7])) - (c[4] * u[4] + c[5] * u[5])) - (c[2] * u[2] + c[3] * u[3]) - (c[0] * u[0] + c[1] * u[1])
         for j in range(0, 8, 2):
-            slope = e[j, j + 1] * reciprocal(e[j, j])
+            slope = e[j, j + 1] * pl.reciprocal(e[j, j], approx=True)
             r[j + 1] = r[j + 1] - slope * r[j]
             w[j + 1] = w[j + 1] - slope * w[j]
             e[j + 1, j + 1] = e[j + 1, j + 1] - slope * e[j, j + 1]
@@ -385,19 +385,18 @@
             new_w = jnp.where(sub == i, w[i], new_w)
             d = jnp.where(sub == i, e[i, i], d)
         q = lax.rsqrt(d)
-        q = q * (1.5 - 0.5 * d * q * q)
         S[k] = jnp.where(lane >= sub + 8 * k, new_s * q, 0.0)
         W[k] = new_w * q
     return jnp.concatenate(S, axis=0), jnp.concatenate(W, axis=0)
 
 
-def chol_kernel(gram_hbm, sample_hbm, basis_ref, tri_ref, gram_ref, sample_ref, sems):
+def chol_kernel(gram_hbm, sample_hbm, basis_ref, tri_ref, gram_ref, sample_ref, spread, sems):
     gram_copy = pltpu.make_async_copy(gram_hbm, gram_ref, sems.at[0])
     sample_copy = pltpu.make_async_copy(sample_hbm, sample_ref, sems.at[1])
     gram_copy.start()
     sample_copy.start()
     gram_copy.wait()
-    R11, V11 = factor_half(gram_ref[:128])
+    R11, V11 = factor_half(gram_ref[:128], spread.at[0])
     R12 = dot(V11, gram_ref[128:256])
     rest = gram_ref[256:] - dot(R12, R12, 0, 0)
     scale = 1.0 / 256
@@ -408,7 +407,7 @@
     tri_ref[:128, :128] = R11 * scale
     tri_ref[:128, 128:] = R12 * scale
     tri_ref[128:, :128] = jnp.zeros((128, 128), jnp.float32)
-    R22, V22 = factor_half(rest)
+    R22, V22 = factor_half(rest, spread.at[1])
     tri_ref[128:, 128:] = R22 * scale
     basis_ref[:, 128:] = dot(second, V22, 1, 1)
 
@@ -419,7 +418,7 @@
         out_shape=(jax.ShapeDtypeStruct((512, 256), jnp.float32), jax.ShapeDtypeStruct((256, 256), jnp.float32)),
         in_specs=[pl.BlockSpec(memory_space=pl.ANY)] * 2,
         out_specs=(pl.BlockSpec(memory_space=pltpu.VMEM),) * 2,
-        scratch_shapes=[pltpu.VMEM((384, 128), jnp.float32), pltpu.VMEM((512, 256), jnp.float32), pltpu.SemaphoreType.DMA((2,))],
+        scratch_shapes=[pltpu.VMEM((384, 128), jnp.float32), pltpu.VMEM((512, 256), jnp.float32), pltpu.VMEM((2, 1280, 128), jnp.float32), pltpu.SemaphoreType.DMA((2,))],
         compiler_params=pltpu.CompilerParams(vmem_limit_bytes=56 << 20),
         name="factor_basis",
     )(gram, values)

time: 108 us -> 107 us (level)
  no operation moved by 1% of the time
where the time goes in v3:
time: 107 us
  Pallas kernels  106 us (99%)
    pallas_call x1, Pallas kernels, sample_and_gram(): pl.pallas_call(sample_kernel, out_shape=(jax.ShapeDtypeStruct((512, 256),...  95.6 us
    pallas_call x1, Pallas kernels, chol(): pl.pallas_call(chol_kernel, out_shape=(jax.ShapeDtypeStruct((512, 256), j...  10.2 us

profile of v3, /device:TPU:1, one launch (start us, length us, event | category | flops | bytes accessed | tf_op | source)
XLA Modules:
  0.0 106.7 jit_solution(13301979522877899959)
XLA Ops:
  0.6 95.6 %sample_gram.1 = (f32[512,256]{1,0:T(8,128)}, f32[384,128]{1,0:T(8,128)}) custom-call(s32[2,48]{1,0:T(2,128)} %cols_ref.1, s32[2]{0:T(128)} %counts_ref.1, bf16[2,48,256,256]{3,2,1,0:T(8,128)(2,1)} %blocks_ref.1, bf16[512,256]{1,0:T(8,128)(2,1)} %panel_ref.1), custom_call_target="tpu_custom_call" | custom-call | tf_op jit(solution)/shard_map/sample_gram/pallas_call | solution.py:287
  96.3 10.2 %factor_basis.1 = (f32[512,256]{1,0:T(8,128)}, f32[256,256]{1,0:T(8,128)}) custom-call(f32[384,128]{1,0:T(8,128)} %get-tuple-element.4.gram_hbm, f32[512,256]{1,0:T(8,128)} %get-tuple-element.5.sample_hbm), custom_call_target="tpu_custom_call" | custom-call | tf_op jit(solution)/shard_map/factor_basis/pallas_call | solution.py:416

commit v4 on v3

--- a/solution.py
+++ b/solution.py
@@ -262,7 +262,14 @@
     for q in PS:
         pairs[q].wait_recv()
         along(0, q, local[part_rows(core, q)] + twin_half[q])
+    for copy in started + pairs:
+        copy.wait_send()
+    sample_copy.wait()
     for t in range(3):
+        if t:
+            for q in PS:
+                for i in (1, 3, 2):
+                    lines[t - 1, q, i].wait_send()
         for q in PS:
             for i in (1, 3, 2):
                 lines[t, q, i].wait_recv()
@@ -270,16 +277,18 @@
             if t < 2:
                 along(t + 1, q, total)
                 continue
-            gram_ref[part_rows(core, q)] = total
+            twin_half[q] = total
+            backs.append(pltpu.make_async_copy(twin_half.at[q], gram_ref.at[part_rows(core, q)], local_sem.at[4 + q]))
+            backs[-1].start()
             backs.append(pltpu.make_async_remote_copy(
-                src_ref=gram_ref.at[part_rows(core, q)], dst_ref=gram_ref.at[part_rows(core, q)], send_sem=pair_send.at[1, q], recv_sem=pair_recv.at[1, q],
+                src_ref=twin_half.at[q], dst_ref=gram_ref.at[part_rows(core, q)], send_sem=pair_send.at[1, q], recv_sem=pair_recv.at[1, q],
                 device_id=(sibling,), device_id_type=MESH))
-            backs[q].start()
+            backs[-1].start()
+    for q in PS:
+        for i in (1, 3, 2):
+            lines[2, q, i].wait_send()
     for copy in backs:
-        copy.wait_recv()
-    for copy in started + list(lines.values()) + pairs + backs:
-        copy.wait_send()
-    sample_copy.wait()
+        copy.wait()
     assert len(started) == N_COPIES, len(started)
 
 
@@ -288,7 +297,7 @@
         sample_kernel,
         out_shape=(jax.ShapeDtypeStruct((512, 256), jnp.float32), jax.ShapeDtypeStruct((384, 128), jnp.float32)),
         in_specs=[pl.BlockSpec(memory_space=pltpu.SMEM)] * 2 + [pl.BlockSpec(memory_space=pl.ANY)] * 2,
-        out_specs=(pl.BlockSpec(memory_space=pl.ANY), pl.BlockSpec(memory_space=pltpu.VMEM)),
+        out_specs=(pl.BlockSpec(memory_space=pl.ANY),) * 2,
         scratch_shapes=[
             pltpu.VMEM((4, 4, 4, 2, 512, 256), jnp.bfloat16),
             pltpu.VMEM((2, 48, 256, 256), jnp.bfloat16),
@@ -300,7 +309,7 @@
             pltpu.VMEM((3, 3, 4, 64, 128), jnp.float32),
             pltpu.SemaphoreType.DMA((N_COPIES,)),
             pltpu.SemaphoreType.DMA((N_COPIES,)),
-            pltpu.SemaphoreType.DMA((4,)),
+            pltpu.SemaphoreType.DMA((7,)),
             pltpu.SemaphoreType.DMA((3, 3, 3)),
             pltpu.SemaphoreType.DMA((3, 3, 3)),
             pltpu.SemaphoreType.DMA((2, 3)),

time: 107 us -> 106 us (level)
  no operation moved by 1% of the time
where the time goes in v4:
time: 106 us
  Pallas kernels  105 us (99%)
    pallas_call x1, Pallas kernels, sample_and_gram(): pl.pallas_call(sample_kernel, out_shape=(jax.ShapeDtypeStruct((512, 256),...  94.8 us
    pallas_call x1, Pallas kernels, chol(): pl.pallas_call(chol_kernel, out_shape=(jax.ShapeDtypeStruct((512, 256), j...  10.2 us

profile of v4, /device:TPU:1, one launch (start us, length us, event | category | flops | bytes accessed | tf_op | source)
XLA Modules:
  0.0 105.8 jit_solution(16171390626250586788)
XLA Ops:
  0.6 94.8 %sample_gram.1 = (f32[512,256]{1,0:T(8,128)}, f32[384,128]{1,0:T(8,128)}) custom-call(s32[2,48]{1,0:T(2,128)} %cols_ref.1, s32[2]{0:T(128)} %counts_ref.1, bf16[2,48,256,256]{3,2,1,0:T(8,128)(2,1)} %blocks_ref.1, bf16[512,256]{1,0:T(8,128)(2,1)} %panel_ref.1), custom_call_target="tpu_custom_call" | custom-call | tf_op jit(solution)/shard_map/sample_gram/pallas_call | solution.py:296
  95.4 10.2 %factor_basis.1 = (f32[512,256]{1,0:T(8,128)}, f32[256,256]{1,0:T(8,128)}) custom-call(f32[384,128]{1,0:T(8,128)} %get-tuple-element.4.gram_hbm, f32[512,256]{1,0:T(8,128)} %get-tuple-element.5.sample_hbm), custom_call_target="tpu_custom_call" | custom-call | tf_op jit(solution)/shard_map/factor_basis/pallas_call | solution.py:425
